TPU v7x, 32 devices: a whole 2x2x4 slice. The times are simulated.
32 devices in a mesh: row: 8 (over z, core), col: 4 (over y, x).
Axes of the slice: x: 2, y: 2, z: 4, core: 2. Of those that a mesh axis runs over, the one named last changes fastest.
Arguments:
- queries: bfloat16 [4096, 2048], P(('row', 'col')), may hold values from -6 to 6
- keys: bfloat16 [4096, 256], P(('row', 'col')), may hold values from -30 to 30
- values: bfloat16 [4096, 256], P(('row', 'col')), may hold values from -6 to 6
Outputs:
- attended: bfloat16 [4096, 2048], P(('row', 'col'))
All inputs are finite; a program needn't handle non-finite values.
Results may differ from a plain program's by a relative error of at most 0.0057.
Values sent between devices are 32-bit elements; how exact they have to be, the bound alone decides.
A program may use at most 128 MiB of HBM per device.

v0:
```python
import math

import jax
import jax.numpy as jnp
import numpy as np
from jax import lax
from jax.sharding import PartitionSpec as P

HD = 64
KV = 4
QH = 32
F = 2080


def entering(array, axis, combine, identity):
    length, index = (lax.axis_size(axis), lax.axis_index(axis))
    everything = jax.tree.map(lambda part: lax.all_gather(part, axis), array)
    start = jax.tree.map(
        lambda part, zero: jnp.broadcast_to(jnp.asarray(zero, part.dtype), part.shape),
        array,
        identity,
    )

    def lap(k, before):
        reached = k < index
        new = combine(before, jax.tree.map(lambda part: part[k], everything))
        return jax.tree.map(lambda a, b: jnp.where(reached, a, b), new, before)

    return lax.fori_loop(0, length, lap, start)


def expand(field):
    width = field.shape[1]
    pieces = []
    for leading in range(width):
        factor = np.full((width - leading,), math.sqrt(2.0), np.float32)
        factor[0] = 1.0
        piece = field[:, leading : leading + 1, :] * field[:, leading:, :]
        pieces.append(piece * jnp.asarray(factor, jnp.float32)[None, :, None])
    return jnp.concatenate(pieces, axis=1)


def add_pairs(earlier, later):
    return (earlier[0] + later[0], earlier[1] + later[1])


def on_device(queries, keys, values):
    rows_here = keys.shape[0]
    per_group = QH // KV
    score_scale = 1.0 / math.sqrt(HD)
    keys_split = keys.reshape(rows_here, KV, HD)
    values_split = values.reshape(rows_here, KV, HD)
    query_split = queries.reshape(rows_here, KV, per_group, HD)
    key_feats = expand(jnp.transpose(keys_split.astype(jnp.float32), (1, 2, 0))).astype(
        jnp.bfloat16
    )
    local_state = jnp.einsum(
        "kft,tkv->fkv", key_feats, values_split, preferred_element_type=jnp.float32
    ).reshape(F, KV * HD)
    unit_rows = jnp.ones((rows_here,), jnp.bfloat16)
    local_count = jnp.einsum("kft,t->fk", key_feats, unit_rows, preferred_element_type=jnp.float32)
    zero_pair = (jnp.zeros_like(local_state), jnp.zeros_like(local_count))
    inner_state, inner_count = entering((local_state, local_count), "col", add_pairs, zero_pair)
    row_state, row_count = lax.psum((local_state, local_count), "col")
    early_state, early_count = entering((row_state, row_count), "row", add_pairs, zero_pair)
    prior_state = inner_state + early_state
    prior_count = inner_count + early_count
    carried_state = prior_state.astype(jnp.bfloat16)
    carried_count = prior_count.astype(jnp.bfloat16)
    causal = lax.broadcasted_iota(jnp.int32, (rows_here, rows_here), 0) >= lax.broadcasted_iota(
        jnp.int32, (rows_here, rows_here), 1
    )

    def one_head(head_index):
        query_group = lax.dynamic_index_in_dim(query_split, head_index, 1, keepdims=False)
        key_head = lax.dynamic_index_in_dim(keys_split, head_index, 1, keepdims=False)
        value_head = lax.dynamic_index_in_dim(values_split, head_index, 1, keepdims=False)
        state_head = lax.dynamic_slice_in_dim(carried_state, head_index * HD, HD, 1)
        count_head = lax.dynamic_index_in_dim(carried_count, head_index, 1, keepdims=False)
        query_feats = expand(
            jnp.transpose(query_group.astype(jnp.float32) * score_scale, (1, 2, 0))
        ).astype(jnp.bfloat16)
        far_num = jnp.einsum(
            "gft,fv->gtv", query_feats, state_head, preferred_element_type=jnp.float32
        )
        far_den = jnp.einsum(
            "gft,f->gt", query_feats, count_head, preferred_element_type=jnp.float32
        )
        scores = (
            jnp.einsum("tgd,ud->gtu", query_group, key_head, preferred_element_type=jnp.float32)
            * score_scale
        )
        weights = jnp.where(causal[None], scores * scores, 0.0)
        near_den = jnp.sum(weights, axis=-1)
        near_num = jnp.einsum(
            "gtu,ud->gtd",
            weights.astype(jnp.bfloat16),
            value_head,
            preferred_element_type=jnp.float32,
        )
        ratio = (far_num + near_num) / jnp.maximum(far_den + near_den, 1.0)[..., None]
        return jnp.transpose(ratio, (1, 0, 2)).reshape(rows_here, per_group * HD)

    heads = lax.map(one_head, jnp.arange(KV, dtype=jnp.int32))
    return jnp.transpose(heads, (1, 0, 2)).reshape(rows_here, QH * HD).astype(jnp.bfloat16)


def solution(mesh):
    placed = (P(("row", "col"), None), P(("row", "col"), None), P(("row", "col"), None))
    return jax.shard_map(
        on_device, mesh=mesh, in_specs=placed, out_specs=P(("row", "col"), None), check_vma=False
    )
```

profile of v0, /device:TPU:0, one launch (start us, length us, event | category | flops | bytes accessed | tf_op | source)
XLA Modules:
  0.0 925.5 jit_solution(10001896829847699883)
XLA Ops:
  43.4 35.7 %concatenate.8 = bf16[4,2080,128]{2,1,0:T(8,128)(2,1)S(1)} concatenate(bf16[4,64,128]{2,1,0:T(8,128)(2,1)S(1)} %multiply_convert_fusion.1, bf16[4,63,128]{2,1,0:T(8,128)(2,1)S(1)} %fusion.162, bf16[4,62,128]{2,1,0:T(8,128)(2,1)S(1)} %fusion.160, bf16[4,61,128]{2,1,0:T(8,128)(2,1)S(1)} %fusion.158, bf16[4,60,128]{2,1,0:T(8,128)(2,1)S(1)} %fusion.156, ...), dimensions={1} | concatenate | bytes 4259840 | tf_op jit(solution)/shard_map/concatenate | solution.py:40
  81.3 3.0 copy.144
  84.3 91.5 %all-gather.5.cloned.1.call-done = f32[4,2080,256]{2,1,0:T(8,128)} async-done(((f32[1,2080,256]{2,1,0:T(8,128)}), f32[4,2080,256]{2,1,0:T(8,128)}) %all-gather.5.cloned.1.call-update) | async-done | bytes 8519696 | tf_op jit(solution)/shard_map/all_gather | solution.py:17
  176.7 73.6 %all-reduce.2.cloned.1.call-done = f32[1,2080,256]{2,1,0:T(8,128)} async-done(((f32[1,2080,256]{2,1,0:T(8,128)}), f32[1,2080,256]{2,1,0:T(8,128)}) %all-reduce.2.cloned.1.call-update) | async-done | bytes 2129936 | tf_op jit(solution)/shard_map/psum | solution.py:64
  252.9 15.8 %psum.15 = f32[1,2080,4]{1,2,0:T(4,128)S(1)} all-reduce(f32[1,2080,4]{1,2,0:T(4,128)S(1)} %bitcast.441), channel_id=1, replica_groups=mesh['row'=8,'col'=4] {'col'}, use_global_device_ids=true, to_apply=%region_3.4 | all-reduce | flops 8320 | bytes 66560 | tf_op jit(solution)/shard_map/psum | solution.py:64
  268.7 8.4 all-gather.1
  277.1 17.2 %all_gather.27 = f32[8,2080,4]{1,2,0:T(4,128)S(1)} all-gather(f32[1,2080,4]{1,2,0:T(4,128)S(1)} %psum.15), channel_id=1, replica_groups=mesh['row'=8,'col'=4] {'row'}, dimensions={0}, use_global_device_ids=true | all-gather | bytes 299520 | tf_op jit(solution)/shard_map/all_gather | solution.py:17
  294.3 14.9 %while.45 = (s32[]{:T(128)}, f32[2080,256]{1,0:T(8,128)}, f32[2080,4]{0,1:T(4,128)S(1)}, s32[]{:T(128)}, f32[4,2080,256]{2,1,0:T(8,128)}, /*index=5*/f32[4,2080,4]{1,2,0:T(4,128)S(1)}, s32[]{:T(128)}, s32[]{:T(128)}) while((s32[]{:T(128)}, f32[2080,256]{1,0:T(8,128)}, f32[2080,4]{0,1:T(4,128)S(1)}, s32[]{:T(128)}, ...), condition=%wide.region_1.2_spmd.clone, body=%wide.region_0.1_spmd.clone.sunk | while | flops 1622404 | bytes 6489723 | solution.py:29
  294.3 3.2 add_select_fusion.8
  297.5 3.9 add_select_fusion.8
  301.4 3.8 add_select_fusion.8
  305.3 3.9 add_select_fusion.8
  309.2 98.3 %all-gather.7.cloned.1.call-done = f32[8,2080,256]{2,1,0:T(8,128)} async-done(((f32[1,2080,256]{2,1,0:T(8,128)}), f32[8,2080,256]{2,1,0:T(8,128)}) %all-gather.7.cloned.1.call-update) | async-done | bytes 17039376 | tf_op jit(solution)/shard_map/all_gather | solution.py:17
  407.5 18.2 %while.46 = (s32[]{:T(128)}, f32[2080,256]{1,0:T(8,128)S(1)}, f32[2080,4]{0,1:T(4,128)S(1)}, s32[]{:T(128)}, f32[8,2080,256]{2,1,0:T(8,128)}, /*index=5*/f32[8,2080,4]{1,2,0:T(4,128)S(1)}, s32[]{:T(128)}, s32[]{:T(128)}) while((s32[]{:T(128)}, f32[2080,256]{1,0:T(8,128)S(1)}, f32[2080,4]{0,1:T(4,128)S(1)}, s32[]{:T(128)}, ...), condition=%wide.region_5.6_spmd.clone, body=%wide.region_4.5_spmd.clone.sunk | while | flops 1622404 | bytes 6489723 | solution.py:29
  425.7 2.8 add_convert_fusion
  432.2 484.7 %while.44 = (s32[]{:T(128)}, bf16[4,128,512]{1,2,0:T(8,128)(2,1)}, s32[4]{0:T(128)S(1)}, bf16[128,4,8,64]{0,3,2,1:T(8,128)(2,1)S(1)}, bf16[2080,256]{0,1:T(8,128...) while((s32[]{:T(128)}, bf16[4,128,512]{1,2,0:T(8,128)(2,1)}, ...), condition=%wide.region_8.9_spmd.clone.clone, body=%wide.region_6.8_spmd.sunk.clone.clone.sunk | while | flops 317964288 | bytes 54151312 | solution.py:104
  458.6 86.7 %concatenate.13 = bf16[8,2080,128]{2,1,0:T(8,128)(2,1)} concatenate(bf16[8,64,128]{2,1,0:T(8,128)(2,1)S(1)} %multiply_convert_fusion.3, bf16[8,63,128]{2,1,0:T(8,128)(2,1)S(1)} %fusion.374, bf16[8,62,128]{2,1,0:T(8,128)(2,1)S(1)} %fusion.375, bf16[8,61,128]{2,1,0:T(8,128)(2,1)S(1)} %fusion.376, bf16[8,60,128]{2,1,0:T(8,128)(2,1)S(1)} %fusion.377, ...), dimensions={1} | concatenate | bytes 8519680 | tf_op jit(solution)/shard_map/while/body/eval_jaxpr/concatenate | solution.py:40
  545.9 3.3 fusion.439
  579.7 86.7 %concatenate.13 = bf16[8,2080,128]{2,1,0:T(8,128)(2,1)} concatenate(bf16[8,64,128]{2,1,0:T(8,128)(2,1)S(1)} %multiply_convert_fusion.3, bf16[8,63,128]{2,1,0:T(8,128)(2,1)S(1)} %fusion.374, bf16[8,62,128]{2,1,0:T(8,128)(2,1)S(1)} %fusion.375, bf16[8,61,128]{2,1,0:T(8,128)(2,1)S(1)} %fusion.376, bf16[8,60,128]{2,1,0:T(8,128)(2,1)S(1)} %fusion.377, ...), dimensions={1} | concatenate | bytes 8519680 | tf_op jit(solution)/shard_map/while/body/eval_jaxpr/concatenate | solution.py:40
  667.1 3.3 fusion.439
  700.9 86.7 %concatenate.13 = bf16[8,2080,128]{2,1,0:T(8,128)(2,1)} concatenate(bf16[8,64,128]{2,1,0:T(8,128)(2,1)S(1)} %multiply_convert_fusion.3, bf16[8,63,128]{2,1,0:T(8,128)(2,1)S(1)} %fusion.374, bf16[8,62,128]{2,1,0:T(8,128)(2,1)S(1)} %fusion.375, bf16[8,61,128]{2,1,0:T(8,128)(2,1)S(1)} %fusion.376, bf16[8,60,128]{2,1,0:T(8,128)(2,1)S(1)} %fusion.377, ...), dimensions={1} | concatenate | bytes 8519680 | tf_op jit(solution)/shard_map/while/body/eval_jaxpr/concatenate | solution.py:40
  788.3 3.3 fusion.439
  822.1 86.7 %concatenate.13 = bf16[8,2080,128]{2,1,0:T(8,128)(2,1)} concatenate(bf16[8,64,128]{2,1,0:T(8,128)(2,1)S(1)} %multiply_convert_fusion.3, bf16[8,63,128]{2,1,0:T(8,128)(2,1)S(1)} %fusion.374, bf16[8,62,128]{2,1,0:T(8,128)(2,1)S(1)} %fusion.375, bf16[8,61,128]{2,1,0:T(8,128)(2,1)S(1)} %fusion.376, bf16[8,60,128]{2,1,0:T(8,128)(2,1)S(1)} %fusion.377, ...), dimensions={1} | concatenate | bytes 8519680 | tf_op jit(solution)/shard_map/while/body/eval_jaxpr/concatenate | solution.py:40
  909.4 3.3 fusion.439
  (1155 shorter events, 175.2 us)
Async XLA Ops:
  6.7 169.2 %all-gather.5.cloned.1.call-start = ((), (), s32[]{:S(2)}) async-start(), calls=%async_computation | async-start | bytes 10649600 | tf_op jit(solution)/shard_map/all_gather | solution.py:17
  9.4 69.7 %copy-start.6 = (bf16[128,256]{0,1:T(8,128)(2,1)}, bf16[128,256]{0,1:T(8,128)(2,1)S(1)}, u32[]{:S(2)}) copy-start(bf16[128,256]{0,1:T(8,128)(2,1)S(1)} %copy.143) | copy-start | bytes 196612
  15.7 19.0 %copy-start.138 = (f32[14]{0:T(128)S(1)}, f32[14]{0:T(128)}, u32[]{:S(2)}) copy-start(f32[14]{0:T(128)} %constant.273.clone) | copy-start | bytes 172
  15.7 19.6 %copy-start.140 = (f32[13]{0:T(128)S(1)}, f32[13]{0:T(128)}, u32[]{:S(2)}) copy-start(f32[13]{0:T(128)} %constant.274.clone) | copy-start | bytes 160
  15.7 20.3 %copy-start.142 = (f32[12]{0:T(128)S(1)}, f32[12]{0:T(128)}, u32[]{:S(2)}) copy-start(f32[12]{0:T(128)} %constant.275.clone) | copy-start | bytes 148
  15.8 20.9 %copy-start.144 = (f32[11]{0:T(128)S(1)}, f32[11]{0:T(128)}, u32[]{:S(2)}) copy-start(f32[11]{0:T(128)} %constant.276.clone) | copy-start | bytes 136
  15.8 21.5 %copy-start.146 = (f32[10]{0:T(128)S(1)}, f32[10]{0:T(128)}, u32[]{:S(2)}) copy-start(f32[10]{0:T(128)} %constant.277.clone) | copy-start | bytes 124
  15.9 22.1 %copy-start.148 = (f32[9]{0:T(128)S(1)}, f32[9]{0:T(128)}, u32[]{:S(2)}) copy-start(f32[9]{0:T(128)} %constant.278.clone) | copy-start | bytes 112
  16.0 22.7 %copy-start.150 = (f32[8]{0:T(128)S(1)}, f32[8]{0:T(128)}, u32[]{:S(2)}) copy-start(f32[8]{0:T(128)} %constant.279.clone) | copy-start | bytes 100
  16.1 23.2 %copy-start.152 = (f32[7]{0:T(128)S(1)}, f32[7]{0:T(128)}, u32[]{:S(2)}) copy-start(f32[7]{0:T(128)} %constant.280.clone) | copy-start | bytes 88
  16.3 23.8 %copy-start.154 = (f32[6]{0:T(128)S(1)}, f32[6]{0:T(128)}, u32[]{:S(2)}) copy-start(f32[6]{0:T(128)} %constant.281.clone) | copy-start | bytes 76
  16.4 24.4 %copy-start.156 = (f32[5]{0:T(128)S(1)}, f32[5]{0:T(128)}, u32[]{:S(2)}) copy-start(f32[5]{0:T(128)} %constant.282.clone) | copy-start | bytes 64
  16.5 24.9 %copy-start.158 = (f32[4]{0:T(128)S(1)}, f32[4]{0:T(128)}, u32[]{:S(2)}) copy-start(f32[4]{0:T(128)} %constant.283.clone) | copy-start | bytes 52
  16.6 25.5 %copy-start.160 = (f32[3]{0:T(128)S(1)}, f32[3]{0:T(128)}, u32[]{:S(2)}) copy-start(f32[3]{0:T(128)} %constant.284.clone) | copy-start | bytes 40
  16.7 26.0 %copy-start.162 = (f32[2]{0:T(128)S(1)}, f32[2]{0:T(128)}, u32[]{:S(2)}) copy-start(f32[2]{0:T(128)} %constant.285.clone) | copy-start | bytes 28
  84.3 166.0 %copy-start.5 = (bf16[128,2048]{1,0:T(8,128)(2,1)S(1)}, bf16[128,2048]{1,0:T(8,128)(2,1)}, u32[]{:S(2)}) copy-start(bf16[128,2048]{1,0:T(8,128)(2,1)} %param.137) | copy-start | bytes 1572868
  175.9 74.4 %all-reduce.2.cloned.1.call-start = ((), (), s32[]{:S(2)}) async-start(), calls=%async_computation.1 | async-start | bytes 4259840 | tf_op jit(solution)/shard_map/psum | solution.py:64
  176.6 230.9 %all-gather.7.cloned.1.call-start = ((), (), s32[]{:S(2)}) async-start(), calls=%async_computation.2 | async-start | bytes 19169280 | tf_op jit(solution)/shard_map/all_gather | solution.py:17
  438.3 18.9 %copy-start.161 = (f32[3]{0:T(128)S(1)}, f32[3]{0:T(128)}, u32[]{:S(2)}) copy-start(f32[3]{0:T(128)} %get-tuple-element.1528) | copy-start | bytes 40 | tf_op jit(solution)/shard_map/while
  438.3 19.6 %copy-start.163 = (f32[2]{0:T(128)S(1)}, f32[2]{0:T(128)}, u32[]{:S(2)}) copy-start(f32[2]{0:T(128)} %get-tuple-element.1529) | copy-start | bytes 28 | tf_op jit(solution)/shard_map/while
  559.5 18.9 %copy-start.161 = (f32[3]{0:T(128)S(1)}, f32[3]{0:T(128)}, u32[]{:S(2)}) copy-start(f32[3]{0:T(128)} %get-tuple-element.1528) | copy-start | bytes 40 | tf_op jit(solution)/shard_map/while
  559.5 19.6 %copy-start.163 = (f32[2]{0:T(128)S(1)}, f32[2]{0:T(128)}, u32[]{:S(2)}) copy-start(f32[2]{0:T(128)} %get-tuple-element.1529) | copy-start | bytes 28 | tf_op jit(solution)/shard_map/while
  680.7 19.6 %copy-start.163 = (f32[2]{0:T(128)S(1)}, f32[2]{0:T(128)}, u32[]{:S(2)}) copy-start(f32[2]{0:T(128)} %get-tuple-element.1529) | copy-start | bytes 28 | tf_op jit(solution)/shard_map/while
  801.8 19.6 %copy-start.163 = (f32[2]{0:T(128)S(1)}, f32[2]{0:T(128)}, u32[]{:S(2)}) copy-start(f32[2]{0:T(128)} %get-tuple-element.1529) | copy-start | bytes 28 | tf_op jit(solution)/shard_map/while
  (352 other events, 2194.9 us)
Sparse Core Ops, SparseCore 0:
  84.4 91.3 all-gather.4
  179.8 70.3 all-reduce.1
  252.0 155.4 all-gather.6
where the time goes:
time: 943 us; the launch traced here: 925 us
  local copies, waits for them, and re-layouts  401 us (43%)
  waiting for transfers between devices  264 us (28%)
  other arithmetic  162 us (17%)
  blocking collectives  41.3 us (4%)
  matrix products  28 us (3%)
  loops' own time  14.8 us (2%)
  between operations  14.5 us (2%)
    concatenate x5, local copies, waits for them, and re-layouts, expand(): return jnp.concatenate(pieces, axis=1)  383 us
    all_gather x2, waiting for transfers between devices, entering(): everything = jax.tree.map(lambda part: lax.all_gather(part, axis), array)  190 us
    another operation x320, other arithmetic  126 us
    psum x1, waiting for transfers between devices, on_device(): row_state, row_count = lax.psum((local_state, local_count), 'col')  73.6 us
    select_n x24, other arithmetic, lap(): return jax.tree.map(lambda a, b: jnp.where(reached, a, b), new, before)  32.8 us
    all_gather x2, blocking collectives, entering(): everything = jax.tree.map(lambda part: lax.all_gather(part, axis), array)  25.5 us
  transfers between devices with their start and end apart: 3, of which 3 were waited for; matrix products, arithmetic and copies ran while one was open for 2% of the time, Pallas kernels for 0%

commit v1 on v0

v1 whole, which is shorter than its diff:
```python
import jax
import jax.numpy as jnp
from jax import lax
from jax.experimental import pallas as pl
from jax.experimental.pallas import tpu as pltpu
from jax.sharding import PartitionSpec as P

HD = 64
KV = 4
QH = 32
PAIRS = QH // KV // 2
LANES = 2 * HD


def paired(tile, odd):
    low = lax.broadcasted_iota(jnp.int32, tile.shape, 1) < HD
    other = pltpu.roll(tile, HD, 1)
    zero = jnp.zeros_like(tile)
    if odd:
        return jnp.where(low, other, zero), jnp.where(low, zero, tile)
    return jnp.where(low, tile, zero), jnp.where(low, zero, other)


def attend_chunk(q_s, k_tiles, v_tiles, acc, masked, tok0, key0):
    keys_here = k_tiles(0).shape[0]
    tokens = q_s.shape[1] // PAIRS
    low = lax.broadcasted_iota(jnp.int32, (keys_here, LANES), 1) < HD
    one_lo = jnp.where(low, 1.0, 0.0).astype(jnp.bfloat16)
    one_hi = jnp.where(low, 0.0, 1.0).astype(jnp.bfloat16)
    for h in range(KV):
        k_lo, k_hi = paired(k_tiles(h // 2), h % 2)
        v_lo, v_hi = paired(v_tiles(h // 2), h % 2)
        kb = jnp.concatenate([k_lo, k_hi], 0).astype(jnp.bfloat16)
        vb = jnp.concatenate(
            [
                jnp.concatenate([v_lo.astype(jnp.bfloat16), one_lo], 1),
                jnp.concatenate([v_hi.astype(jnp.bfloat16), one_hi], 1),
            ],
            0,
        )
        s = lax.dot_general(
            q_s[h], kb, (((1,), (1,)), ((), ())), preferred_element_type=jnp.float32
        )
        if masked:
            tok = tok0 + lax.broadcasted_iota(jnp.int32, s.shape, 0) % tokens
            key = key0 + lax.broadcasted_iota(jnp.int32, s.shape, 1) % keys_here
            s = jnp.where(key <= tok, s, 0.0)
        w = (s * s).astype(jnp.bfloat16)
        acc[h] += jnp.dot(w, vb, preferred_element_type=jnp.float32)


def kernel(me_ref, q_ref, k_ref, v_ref, o_ref, q_s, acc):
    tokens = q_ref.shape[0]
    chunk = k_ref.shape[0]
    step = pl.program_id(0)
    tok0 = me_ref[0] * tokens
    last = tok0 // chunk

    @pl.when(step == 0)
    def _():
        for h in range(KV):
            for p in range(PAIRS):
                q_s[h, p * tokens : (p + 1) * tokens, :] = (
                    q_ref[:, (h * PAIRS + p) * LANES : (h * PAIRS + p + 1) * LANES].astype(
                        jnp.float32
                    )
                    * 0.125
                ).astype(jnp.bfloat16)
        acc[...] = jnp.zeros_like(acc)

    def k_tiles(i):
        return k_ref[:, i * LANES : (i + 1) * LANES]

    def v_tiles(i):
        return v_ref[:, i * LANES : (i + 1) * LANES]

    @pl.when(step < last)
    def _():
        attend_chunk(q_s, k_tiles, v_tiles, acc, False, 0, 0)

    @pl.when(step == last)
    def _():
        attend_chunk(q_s, k_tiles, v_tiles, acc, True, tok0, last * chunk)
        for h in range(KV):
            for p in range(PAIRS):
                part = acc[h, p * tokens : (p + 1) * tokens, :]
                o_ref[:, (h * PAIRS + p) * LANES : (h * PAIRS + p + 1) * LANES] = (
                    part[:, :LANES] / jnp.maximum(part[:, LANES:], 1.0)
                ).astype(jnp.bfloat16)


def on_device(queries, keys, values):
    axes = ("row", "col")
    tokens = queries.shape[0]
    me = (lax.axis_index("row") * lax.axis_size("col") + lax.axis_index("col")).reshape(1)
    both = jnp.concatenate([keys, values], 1).astype(jnp.float32)
    every = lax.all_gather(both, axes, axis=0, tiled=True)
    total = every.shape[0]
    chunk = 4 * tokens
    width = KV * HD
    return pl.pallas_call(
        kernel,
        out_shape=jax.ShapeDtypeStruct(queries.shape, jnp.bfloat16),
        grid_spec=pltpu.PrefetchScalarGridSpec(
            num_scalar_prefetch=1,
            grid=(total // chunk,),
            in_specs=[
                pl.BlockSpec(queries.shape, lambda s, m: (0, 0)),
                pl.BlockSpec((chunk, width), lambda s, m: (jnp.minimum(s, m[0] // 4), 0)),
                pl.BlockSpec((chunk, width), lambda s, m: (jnp.minimum(s, m[0] // 4), 1)),
            ],
            out_specs=pl.BlockSpec(queries.shape, lambda s, m: (0, 0)),
            scratch_shapes=[
                pltpu.VMEM((KV, PAIRS * tokens, LANES), jnp.bfloat16),
                pltpu.VMEM((KV, PAIRS * tokens, 2 * LANES), jnp.float32),
            ],
        ),
        compiler_params=pltpu.CompilerParams(vmem_limit_bytes=40 * 2**20),
    )(me, queries, every, every)


def solution(mesh):
    placed = P(("row", "col"), None)
    return jax.shard_map(
        on_device, mesh=mesh, in_specs=(placed,) * 3, out_specs=placed, check_vma=False
    )
```

time: 943 us -> 121 us (0.13)
  the two profiles are of different devices: /device:TPU:0 before, /device:TPU:25 now
where the time goes in v1:
time: 121 us
  waiting for transfers between devices  79.6 us (66%)
  Pallas kernels  21.7 us (18%)
  between operations  13.4 us (11%)
  local copies, waits for them, and re-layouts  4.42 us (4%)
  other arithmetic  1.6 us (1%)
    all_gather x1, waiting for transfers between devices, on_device(): every = lax.all_gather(both, axes, axis=0, tiled=True)  79.6 us
    pallas_call x1, Pallas kernels, on_device(): pl.pallas_call(kernel, out_shape=jax.ShapeDtypeStruct(queries.shape, jnp....  21.7 us
    unnamed x4, local copies, waits for them, and re-layouts  4.42 us
  transfers between devices with their start and end apart: 1, of which 1 were waited for; matrix products, arithmetic and copies ran while one was open for 0% of the time, Pallas kernels for 0%

profile of v1, /device:TPU:25, one launch (start us, length us, event | category | flops | bytes accessed | tf_op | source)
XLA Modules:
  0.0 120.8 jit_solution(17969171242835573941)
XLA Ops:
  6.5 0.0 all-gather.2.cloned.1.call-start
  6.5 1.6 %maximum_convert_fusion = f32[128,512]{1,0:T(8,128)} fusion(bf16[128,256]{1,0:T(8,128)(2,1)} %param.5, bf16[128,256]{1,0:T(8,128)(2,1)} %param.4), kind=kLoop, calls=%fused_computation | loop fusion | flops 262144 | bytes 393216 | tf_op jit(solution)/shard_map/convert_element_type | solution.py:96
  8.1 0.0 all-gather.2.cloned.1.call-update
  8.2 79.6 %all-gather.2.cloned.1.call-done.k_ref.v_ref = f32[4096,512]{1,0:T(8,128)} async-done(((f32[128,512]{1,0:T(8,128)}), f32[4096,512]{1,0:T(8,128)}) %all-gather.2.cloned.1.call-update) | async-done | bytes 8388624 | tf_op jit(solution)/shard_map/all_gather | solution.py:97
  87.8 0.0 copy-start
  87.8 3.4 %copy-done = f32[4096,512]{1,0:T(8,128)S(1)} copy-done((f32[4096,512]{1,0:T(8,128)S(1)}, f32[4096,512]{1,0:T(8,128)}, u32[]{:S(2)}) %copy-start) | copy-done | bytes 8388632
  91.2 0.0 copy-start.1
  91.2 1.0 copy-done.1
  92.2 21.7 %shard_map.37 = bf16[128,2048]{1,0:T(8,128)(2,1)} custom-call(s32[1]{0:T(128)} %bitcast.me_ref, bf16[128,2048]{1,0:T(8,128)(2,1)S(1)} %copy-done.1, f32[4096,512]{1,0:T(8,128)S(1)} %copy-done, f32[4096,512]{1,0:T(8,128)S(1)} %copy-done), custom_call_target="tpu_custom_call" | custom-call | tf_op jit(solution)/shard_map/pallas_call | solution.py:101
Async XLA Ops:
  6.5 81.3 %all-gather.2.cloned.1.call-start = ((), (), s32[]{:S(2)}) async-start(), calls=%async_computation | async-start | bytes 8650752 | tf_op jit(solution)/shard_map/all_gather | solution.py:97
  87.8 3.4 %copy-start = (f32[4096,512]{1,0:T(8,128)S(1)}, f32[4096,512]{1,0:T(8,128)}, u32[]{:S(2)}) copy-start(f32[4096,512]{1,0:T(8,128)} %all-gather.2.cloned.1.call-done.k_ref.v_ref) | copy-start | bytes 25165828
  91.2 1.0 copy-start.1
Sparse Core Ops, SparseCore 0:
  10.2 77.5 all-gather.1

commit v2 on v1

--- a/solution.py
+++ b/solution.py
@@ -1,3 +1,5 @@
+import functools
+
 import jax
 import jax.numpy as jnp
 from jax import lax
@@ -119,8 +121,224 @@
     )(me, queries, every, every)
 
 
+def fused_kernel(axes, shape, q_ref, k_ref, v_ref, o_ref, q_s, acc, held, send, recv):
+    rows, cols = shape
+    levels = rows // 2
+    tokens = q_ref.shape[0]
+    width = k_ref.shape[1]
+    row, col = lax.axis_index(axes[0]), lax.axis_index(axes[1])
+    z, c = row // 2, row % 2
+    x, y = col % 2, col // 2
+    x_col = y * 2 + 1 - x
+    y_col = (1 - y) * 2 + x
+    d_col = 3 - col
+    x_dev, y_dev = (row, x_col), (row, y_col)
+    core_dev = (z * 2 + 1 - c, col)
+    up_dev, down_dev = (row + 2, col), (row - 2, col)
+    not_top = z < levels - 1
+
+    barrier = pltpu.get_barrier_semaphore()
+
+    def greet(dev):
+        pl.semaphore_signal(barrier, inc=1, device_id=dev, device_id_type=pl.DeviceIdType.MESH)
+
+    for dev in (x_dev, y_dev, core_dev):
+        greet(dev)
+
+    @pl.when(not_top)
+    def _():
+        greet(up_dev)
+
+    @pl.when(z > 0)
+    def _():
+        greet(down_dev)
+
+    me = row * cols + col
+    held[me, 0] = k_ref[...].astype(jnp.float32)
+    held[me, 1] = v_ref[...].astype(jnp.float32)
+
+    pl.semaphore_wait(barrier, 3 + jnp.minimum(z, 1) + jnp.minimum(levels - 1 - z, 1))
+
+    def block(level, core, column):
+        return (2 * (z - level) + core) * cols + column
+
+    def whole(level, kind, b, dev):
+        return pltpu.make_async_remote_copy(
+            src_ref=held.at[b],
+            dst_ref=held.at[b],
+            send_sem=send.at[level, kind],
+            recv_sem=recv.at[b, 0],
+            device_id=dev,
+            device_id_type=pl.DeviceIdType.MESH,
+        )
+
+    def piece(level, kind, b, part, dev):
+        return pltpu.make_async_remote_copy(
+            src_ref=held.at[b, part],
+            dst_ref=held.at[b, part],
+            send_sem=send.at[level, kind],
+            recv_sem=recv.at[b, part],
+            device_id=dev,
+            device_id_type=pl.DeviceIdType.MESH,
+        )
+
+    def up_copy(level):
+        return whole(level, 0, block(level, c, col), up_dev)
+
+    def across(level):
+        own = block(level, c, col)
+        return whole(level, 1, own, x_dev), whole(level, 2, own, y_dev)
+
+    def corner(level):
+        return (
+            piece(level, 3, block(level, c, x_col), 0, y_dev),
+            piece(level, 4, block(level, c, y_col), 1, x_dev),
+        )
+
+    def to_core(level, which):
+        column = (col, x_col, y_col, d_col)[which]
+        return whole(level, 5 + which, block(level, c, column), core_dev)
+
+    def own_sends(level):
+        for copy in across(level):
+            copy.start()
+
+        @pl.when(not_top)
+        def _():
+            up_copy(level).start()
+
+        @pl.when((level > 0) | (c == 0))
+        def _():
+            to_core(level, 0).start()
+
+    def chunk(r, masked):
+        def k_tiles(i):
+            t = held[pl.ds(r * cols, cols), 0, :, i * LANES : (i + 1) * LANES]
+            return t.reshape(cols * tokens, LANES)
+
+        def v_tiles(i):
+            t = held[pl.ds(r * cols, cols), 1, :, i * LANES : (i + 1) * LANES]
+            return t.reshape(cols * tokens, LANES)
+
+        attend_chunk(q_s, k_tiles, v_tiles, acc, masked, col * tokens, 0)
+
+    own_sends(0)
+    for h in range(KV):
+        for p in range(PAIRS):
+            q_s[h, p * tokens : (p + 1) * tokens, :] = (
+                q_ref[:, (h * PAIRS + p) * LANES : (h * PAIRS + p + 1) * LANES].astype(jnp.float32)
+                * 0.125
+            ).astype(jnp.bfloat16)
+    acc[...] = jnp.zeros_like(acc)
+
+    def lap(level, _):
+        inside = level <= z
+
+        @pl.when(inside)
+        def _():
+            own = block(level, c, col)
+            whole(level, 1, block(level, c, x_col), x_dev).wait_recv()
+            whole(level, 2, block(level, c, y_col), y_dev).wait_recv()
+            for copy in corner(level):
+                copy.start()
+
+            @pl.when((level > 0) | (c == 0))
+            def _():
+                to_core(level, 1).start()
+                to_core(level, 2).start()
+
+        @pl.when(level < z)
+        def _():
+            whole(level + 1, 0, block(level + 1, c, col), down_dev).wait_recv()
+            own_sends(level + 1)
+
+        @pl.when((level > 1) | ((level == 1) & (c == 1)))
+        def _():
+            for column in range(cols):
+                whole(level - 1, 5, block(level - 1, 1 - c, column), core_dev).wait_recv()
+            chunk(2 * (z - level + 1) + 1 - c, False)
+
+        @pl.when(inside)
+        def _():
+            b = block(level, c, d_col)
+            piece(level, 3, b, 0, y_dev).wait_recv()
+            piece(level, 4, b, 1, x_dev).wait_recv()
+
+            @pl.when((level > 0) | (c == 0))
+            def _():
+                to_core(level, 3).start()
+
+        @pl.when(level == 0)
+        def _():
+            chunk(row, True)
+
+        @pl.when(inside & (level > 0))
+        def _():
+            chunk(2 * (z - level) + c, False)
+
+        return 0
+
+    lax.fori_loop(0, z + 2, lap, 0)
+
+    for h in range(KV):
+        for p in range(PAIRS):
+            part = acc[h, p * tokens : (p + 1) * tokens, :]
+            o_ref[:, (h * PAIRS + p) * LANES : (h * PAIRS + p + 1) * LANES] = (
+                part[:, :LANES] / jnp.maximum(part[:, LANES:], 1.0)
+            ).astype(jnp.bfloat16)
+
+    def drain(level, _):
+        for copy in across(level) + corner(level):
+            copy.wait_send()
+
+        @pl.when(not_top)
+        def _():
+            up_copy(level).wait_send()
+
+        @pl.when((level > 0) | (c == 0))
+        def _():
+            for which in range(4):
+                to_core(level, which).wait_send()
+
+        return 0
+
+    lax.fori_loop(0, z + 1, drain, 0)
+
+
+def fused(shape, queries, keys, values):
+    tokens, width = keys.shape
+    rows, cols = shape
+    in_vmem = pl.BlockSpec(memory_space=pltpu.VMEM)
+    return pl.pallas_call(
+        functools.partial(fused_kernel, ("row", "col"), shape),
+        out_shape=jax.ShapeDtypeStruct(queries.shape, jnp.bfloat16),
+        in_specs=[in_vmem] * 3,
+        out_specs=in_vmem,
+        scratch_shapes=[
+            pltpu.VMEM((KV, PAIRS * tokens, LANES), jnp.bfloat16),
+            pltpu.VMEM((KV, PAIRS * tokens, 2 * LANES), jnp.float32),
+            pltpu.VMEM((rows * cols, 2, tokens, width), jnp.float32),
+            pltpu.SemaphoreType.DMA((rows // 2, 9)),
+            pltpu.SemaphoreType.DMA((rows * cols, 2)),
+        ],
+        compiler_params=pltpu.CompilerParams(
+            collective_id=0, has_side_effects=True, vmem_limit_bytes=40 * 2**20
+        ),
+    )(queries, keys, values)
+
+
 def solution(mesh):
     placed = P(("row", "col"), None)
-    return jax.shard_map(
-        on_device, mesh=mesh, in_specs=(placed,) * 3, out_specs=placed, check_vma=False
-    )
+    rows, cols = mesh.shape["row"], mesh.shape["col"]
+
+    def whole(queries, keys, values):
+        held_bytes = keys.size * 8
+        if cols == 4 and rows % 2 == 0 and held_bytes <= 16 * 2**20:
+            local = functools.partial(fused, (rows, cols))
+        else:
+            local = on_device
+        return jax.shard_map(
+            local, mesh=mesh, in_specs=(placed,) * 3, out_specs=placed, check_vma=False
+        )(queries, keys, values)
+
+    return whole

time: 121 us -> 51.5 us (0.43)
  the two profiles are of different devices: /device:TPU:25 before, /device:TPU:24 now
where the time goes in v2:
time: 51.5 us; the launch traced here: 51.3 us
  Pallas kernels  47.8 us (93%)
  local copies, waits for them, and re-layouts  3.51 us (7%)
    pallas_call x1, Pallas kernels, fused(): pl.pallas_call(functools.partial(fused_kernel, ('row', 'col'), shape), ou...  47.8 us
    unnamed x7, local copies, waits for them, and re-layouts  3.51 us

profile of v2, /device:TPU:24, one launch (start us, length us, event | category | flops | bytes accessed | tf_op | source)
XLA Modules:
  0.0 51.3 jit_solution(12267319395974802052)
XLA Ops:
  0.0 0.0 copy-start
  0.0 1.0 %copy-done = bf16[128,2048]{1,0:T(8,128)(2,1)S(1)} copy-done((bf16[128,2048]{1,0:T(8,128)(2,1)S(1)}, bf16[128,2048]{1,0:T(8,128)(2,1)}, u32[]{:S(2)}) %copy-start) | copy-done | bytes 524312
  1.0 0.0 copy-start.1
  1.0 0.8 %copy-done.1 = bf16[128,256]{1,0:T(8,128)(2,1)S(1)} copy-done((bf16[128,256]{1,0:T(8,128)(2,1)S(1)}, bf16[128,256]{1,0:T(8,128)(2,1)}, u32[]{:S(2)}) %copy-start.1) | copy-done | bytes 65560
  1.9 0.0 copy-start.2
  1.9 0.8 %copy-done.2 = bf16[128,256]{1,0:T(8,128)(2,1)S(1)} copy-done((bf16[128,256]{1,0:T(8,128)(2,1)S(1)}, bf16[128,256]{1,0:T(8,128)(2,1)}, u32[]{:S(2)}) %copy-start.2) | copy-done | bytes 65560
  2.7 47.8 %shard_map.37 = bf16[128,2048]{1,0:T(8,128)(2,1)S(1)} custom-call(bf16[128,2048]{1,0:T(8,128)(2,1)S(1)} %copy-done, bf16[128,256]{1,0:T(8,128)(2,1)S(1)} %copy-done.1, bf16[128,256]{1,0:T(8,128)(2,1)S(1)} %copy-done.2), custom_call_target="tpu_custom_call" | custom-call | tf_op jit(solution)/shard_map/pallas_call | solution.py:312
  50.5 0.8 %copy.5 = bf16[128,2048]{1,0:T(8,128)(2,1)} copy(bf16[128,2048]{1,0:T(8,128)(2,1)S(1)} %shard_map.37) | data formatting | bytes 1048576
Async XLA Ops:
  0.0 1.0 %copy-start = (bf16[128,2048]{1,0:T(8,128)(2,1)S(1)}, bf16[128,2048]{1,0:T(8,128)(2,1)}, u32[]{:S(2)}) copy-start(bf16[128,2048]{1,0:T(8,128)(2,1)} %q_ref.1) | copy-start | bytes 1572868
  1.0 0.8 %copy-start.1 = (bf16[128,256]{1,0:T(8,128)(2,1)S(1)}, bf16[128,256]{1,0:T(8,128)(2,1)}, u32[]{:S(2)}) copy-start(bf16[128,256]{1,0:T(8,128)(2,1)} %k_ref.1) | copy-start | bytes 196612
  1.9 0.8 %copy-start.2 = (bf16[128,256]{1,0:T(8,128)(2,1)S(1)}, bf16[128,256]{1,0:T(8,128)(2,1)}, u32[]{:S(2)}) copy-start(bf16[128,256]{1,0:T(8,128)(2,1)} %v_ref.1) | copy-start | bytes 196612

commit v3 on v2

--- a/solution.py
+++ b/solution.py
@@ -121,7 +121,9 @@
     )(me, queries, every, every)
 
 
-def fused_kernel(axes, shape, q_ref, k_ref, v_ref, o_ref, q_s, acc, held, send, recv):
+def fused_kernel(
+    axes, shape, q_hbm, k_hbm, v_hbm, o_ref, q_ref, k_ref, v_ref, q_s, acc, held, local, send, recv
+):
     rows, cols = shape
     levels = rows // 2
     tokens = q_ref.shape[0]
@@ -137,6 +139,12 @@
     up_dev, down_dev = (row + 2, col), (row - 2, col)
     not_top = z < levels - 1
 
+    loads = [
+        pltpu.make_async_copy(src, dst, local.at[i])
+        for i, (src, dst) in enumerate(((k_hbm, k_ref), (v_hbm, v_ref), (q_hbm, q_ref)))
+    ]
+    for load in loads:
+        load.start()
     barrier = pltpu.get_barrier_semaphore()
 
     def greet(dev):
@@ -154,6 +162,8 @@
         greet(down_dev)
 
     me = row * cols + col
+    loads[0].wait()
+    loads[1].wait()
     held[me, 0] = k_ref[...].astype(jnp.float32)
     held[me, 1] = v_ref[...].astype(jnp.float32)
 
@@ -211,18 +221,34 @@
         def _():
             to_core(level, 0).start()
 
-    def chunk(r, masked):
-        def k_tiles(i):
-            t = held[pl.ds(r * cols, cols), 0, :, i * LANES : (i + 1) * LANES]
-            return t.reshape(cols * tokens, LANES)
-
-        def v_tiles(i):
-            t = held[pl.ds(r * cols, cols), 1, :, i * LANES : (i + 1) * LANES]
-            return t.reshape(cols * tokens, LANES)
-
-        attend_chunk(q_s, k_tiles, v_tiles, acc, masked, col * tokens, 0)
+    def chunk(first, second, masked):
+        def tiles(part, i):
+            lanes = slice(i * LANES, (i + 1) * LANES)
+            halves = [
+                held[pl.ds(b, 2), part, :, lanes].reshape(2 * tokens, LANES)
+                for b in (first, second)
+            ]
+            return jnp.concatenate(halves, 0)
+
+        attend_chunk(
+            q_s,
+            lambda i: tiles(0, i),
+            lambda i: tiles(1, i),
+            acc,
+            masked,
+            col * tokens,
+            0,
+        )
+
+    def core_arrival(level, column):
+        whole(level, 5, block(level, 1 - c, column), core_dev).wait_recv()
+
+    def from_below(level):
+        whole(level, 0, block(level, c, col), down_dev).wait_recv()
+        own_sends(level)
 
     own_sends(0)
+    loads[2].wait()
     for h in range(KV):
         for p in range(PAIRS):
             q_s[h, p * tokens : (p + 1) * tokens, :] = (
@@ -236,7 +262,6 @@
 
         @pl.when(inside)
         def _():
-            own = block(level, c, col)
             whole(level, 1, block(level, c, x_col), x_dev).wait_recv()
             whole(level, 2, block(level, c, y_col), y_dev).wait_recv()
             for copy in corner(level):
@@ -247,16 +272,24 @@
                 to_core(level, 1).start()
                 to_core(level, 2).start()
 
-        @pl.when(level < z)
-        def _():
-            whole(level + 1, 0, block(level + 1, c, col), down_dev).wait_recv()
-            own_sends(level + 1)
+        @pl.when((level == 0) & (z > 0))
+        def _():
+            from_below(1)
 
         @pl.when((level > 1) | ((level == 1) & (c == 1)))
         def _():
-            for column in range(cols):
-                whole(level - 1, 5, block(level - 1, 1 - c, column), core_dev).wait_recv()
-            chunk(2 * (z - level + 1) + 1 - c, False)
+            core_arrival(level - 1, y_col)
+            core_arrival(level - 1, d_col)
+
+            @pl.when(level == 1)
+            def _():
+                core_arrival(0, col)
+                core_arrival(0, x_col)
+
+            far = 2 * (1 - y)
+            first = jnp.where(level == 1, block(0, 1 - c, 0), block(level - 1, c, far))
+            second = jnp.where(level == 1, block(0, 1 - c, 2), block(level - 1, 1 - c, far))
+            chunk(first, second, False)
 
         @pl.when(inside)
         def _():
@@ -270,11 +303,17 @@
 
         @pl.when(level == 0)
         def _():
-            chunk(row, True)
+            chunk(row * cols, row * cols + 2, True)
 
         @pl.when(inside & (level > 0))
         def _():
-            chunk(2 * (z - level) + c, False)
+            core_arrival(level, col)
+            core_arrival(level, x_col)
+            chunk(block(level, c, 2 * y), block(level, 1 - c, 2 * y), False)
+
+        @pl.when(level + 2 <= z)
+        def _():
+            from_below(level + 2)
 
         return 0
 
@@ -312,17 +351,21 @@
     return pl.pallas_call(
         functools.partial(fused_kernel, ("row", "col"), shape),
         out_shape=jax.ShapeDtypeStruct(queries.shape, jnp.bfloat16),
-        in_specs=[in_vmem] * 3,
+        in_specs=[pl.BlockSpec(memory_space=pltpu.HBM)] * 3,
         out_specs=in_vmem,
         scratch_shapes=[
+            pltpu.VMEM(queries.shape, jnp.bfloat16),
+            pltpu.VMEM(keys.shape, jnp.bfloat16),
+            pltpu.VMEM(values.shape, jnp.bfloat16),
             pltpu.VMEM((KV, PAIRS * tokens, LANES), jnp.bfloat16),
             pltpu.VMEM((KV, PAIRS * tokens, 2 * LANES), jnp.float32),
             pltpu.VMEM((rows * cols, 2, tokens, width), jnp.float32),
+            pltpu.SemaphoreType.DMA((3,)),
             pltpu.SemaphoreType.DMA((rows // 2, 9)),
             pltpu.SemaphoreType.DMA((rows * cols, 2)),
         ],
         compiler_params=pltpu.CompilerParams(
-            collective_id=0, has_side_effects=True, vmem_limit_bytes=40 * 2**20
+            collective_id=0, has_side_effects=True, vmem_limit_bytes=60 * 2**20
         ),
     )(queries, keys, values)
 

time: 51.5 us -> 54.2 us (1.052)
  Pallas kernels: 47.8 us -> 52.1 us
  local copies, waits for them, and re-layouts: 3.51 us -> 1.88 us
    pallas_call x1, Pallas kernels: 47.8 us -> 52.1 us  [fused(): pl.pallas_call(functools.partial(fused_kernel, ('row', 'col'), shape), ou...]
    unnamed x7 -> x1, local copies, waits for them, and re-layouts: 3.51 us -> 1.88 us
where the time goes in v3:
time: 54.2 us; the launch traced here: 54 us
  Pallas kernels  52.1 us (96%)
  local copies, waits for them, and re-layouts  1.88 us (3%)
    pallas_call x1, Pallas kernels, fused(): pl.pallas_call(functools.partial(fused_kernel, ('row', 'col'), shape), ou...  52.1 us
    unnamed x1, local copies, waits for them, and re-layouts  1.88 us

profile of v3, /device:TPU:24, one launch (start us, length us, event | category | flops | bytes accessed | tf_op | source)
XLA Modules:
  0.0 54.0 jit_solution(11316628776165325976)
XLA Ops:
  0.0 52.1 %shard_map.37 = bf16[128,2048]{1,0:T(8,128)(2,1)} custom-call(bf16[128,2048]{1,0:T(8,128)(2,1)} %q_hbm.1, bf16[128,256]{1,0:T(8,128)(2,1)} %k_hbm.1, bf16[128,256]{1,0:T(8,128)(2,1)} %v_hbm.1), custom_call_target="tpu_custom_call" | custom-call | tf_op jit(solution)/shard_map/pallas_call | solution.py:351
  52.1 1.9 %copy.5 = bf16[128,2048]{1,0:T(8,128)(2,1)} copy(bf16[128,2048]{1,0:T(8,128)(2,1)} %shard_map.37) | data formatting | bytes 1048576

commit v4 on v3

--- a/solution.py
+++ b/solution.py
@@ -197,7 +197,12 @@
 
     def across(level):
         own = block(level, c, col)
-        return whole(level, 1, own, x_dev), whole(level, 2, own, y_dev)
+        return (
+            piece(level, 1, own, 0, x_dev),
+            piece(level, 2, own, 1, y_dev),
+            piece(level, 9, own, 1, x_dev),
+            piece(level, 10, own, 0, y_dev),
+        )
 
     def corner(level):
         return (
@@ -262,34 +267,45 @@
 
         @pl.when(inside)
         def _():
-            whole(level, 1, block(level, c, x_col), x_dev).wait_recv()
-            whole(level, 2, block(level, c, y_col), y_dev).wait_recv()
+            piece(level, 1, block(level, c, x_col), 0, x_dev).wait_recv()
+            piece(level, 2, block(level, c, y_col), 1, y_dev).wait_recv()
             for copy in corner(level):
                 copy.start()
+
+        @pl.when(level < z)
+        def _():
+            from_below(level + 1)
+
+        @pl.when((level > 1) | ((level == 1) & (c == 1)))
+        def _():
+            core_arrival(level - 1, y_col)
+            core_arrival(level - 1, d_col)
+
+            @pl.when(level == 1)
+            def _():
+                core_arrival(0, col)
+                core_arrival(0, x_col)
+
+            far = 2 * (1 - y)
+            first = jnp.where(level == 1, block(0, 1 - c, 0), block(level - 1, c, far))
+            second = jnp.where(level == 1, block(0, 1 - c, 2), block(level - 1, 1 - c, far))
+            chunk(first, second, False)
+
+        @pl.when(inside)
+        def _():
+            piece(level, 9, block(level, c, x_col), 1, x_dev).wait_recv()
+            piece(level, 10, block(level, c, y_col), 0, y_dev).wait_recv()
 
             @pl.when((level > 0) | (c == 0))
             def _():
                 to_core(level, 1).start()
                 to_core(level, 2).start()
 
-        @pl.when((level == 0) & (z > 0))
-        def _():
-            from_below(1)
-
-        @pl.when((level > 1) | ((level == 1) & (c == 1)))
-        def _():
-            core_arrival(level - 1, y_col)
-            core_arrival(level - 1, d_col)
-
-            @pl.when(level == 1)
-            def _():
-                core_arrival(0, col)
-                core_arrival(0, x_col)
-
-            far = 2 * (1 - y)
-            first = jnp.where(level == 1, block(0, 1 - c, 0), block(level - 1, c, far))
-            second = jnp.where(level == 1, block(0, 1 - c, 2), block(level - 1, 1 - c, far))
-            chunk(first, second, False)
+        @pl.when(inside & (level > 0))
+        def _():
+            core_arrival(level, col)
+            core_arrival(level, x_col)
+            chunk(block(level, c, 2 * y), block(level, 1 - c, 2 * y), False)
 
         @pl.when(inside)
         def _():
@@ -304,16 +320,6 @@
         @pl.when(level == 0)
         def _():
             chunk(row * cols, row * cols + 2, True)
-
-        @pl.when(inside & (level > 0))
-        def _():
-            core_arrival(level, col)
-            core_arrival(level, x_col)
-            chunk(block(level, c, 2 * y), block(level, 1 - c, 2 * y), False)
-
-        @pl.when(level + 2 <= z)
-        def _():
-            from_below(level + 2)
 
         return 0
 
@@ -361,7 +367,7 @@
             pltpu.VMEM((KV, PAIRS * tokens, 2 * LANES), jnp.float32),
             pltpu.VMEM((rows * cols, 2, tokens, width), jnp.float32),
             pltpu.SemaphoreType.DMA((3,)),
-            pltpu.SemaphoreType.DMA((rows // 2, 9)),
+            pltpu.SemaphoreType.DMA((rows // 2, 11)),
             pltpu.SemaphoreType.DMA((rows * cols, 2)),
         ],
         compiler_params=pltpu.CompilerParams(

time: 54.2 us -> 47.1 us (0.87)
  Pallas kernels: 52.1 us -> 45 us
    pallas_call x1, Pallas kernels: 52.1 us -> 45 us  [fused(): pl.pallas_call(functools.partial(fused_kernel, ('row', 'col'), shape), ou...]
where the time goes in v4:
time: 47.1 us; the launch traced here: 46.9 us
  Pallas kernels  45 us (96%)
  local copies, waits for them, and re-layouts  1.88 us (4%)
    pallas_call x1, Pallas kernels, fused(): pl.pallas_call(functools.partial(fused_kernel, ('row', 'col'), shape), ou...  45 us
    unnamed x1, local copies, waits for them, and re-layouts  1.88 us

profile of v4, /device:TPU:24, one launch (start us, length us, event | category | flops | bytes accessed | tf_op | source)
XLA Modules:
  0.0 46.9 jit_solution(2473686782488765806)
XLA Ops:
  0.0 45.0 %shard_map.37 = bf16[128,2048]{1,0:T(8,128)(2,1)} custom-call(bf16[128,2048]{1,0:T(8,128)(2,1)} %q_hbm.1, bf16[128,256]{1,0:T(8,128)(2,1)} %k_hbm.1, bf16[128,256]{1,0:T(8,128)(2,1)} %v_hbm.1), custom_call_target="tpu_custom_call" | custom-call | tf_op jit(solution)/shard_map/pallas_call | solution.py:357
  45.0 1.9 %copy.5 = bf16[128,2048]{1,0:T(8,128)(2,1)} copy(bf16[128,2048]{1,0:T(8,128)(2,1)} %shard_map.37) | data formatting | bytes 1048576

commit v5 on v4

--- a/solution.py
+++ b/solution.py
@@ -215,12 +215,12 @@
         return whole(level, 5 + which, block(level, c, column), core_dev)
 
     def own_sends(level):
+        @pl.when(not_top)
+        def _():
+            up_copy(level).start()
+
         for copy in across(level):
             copy.start()
-
-        @pl.when(not_top)
-        def _():
-            up_copy(level).start()
 
         @pl.when((level > 0) | (c == 0))
         def _():

time: 47.1 us -> 47.1 us (level)
  no operation moved by 1% of the time
where the time goes in v5:
time: 47.1 us; the launch traced here: 46.9 us
  Pallas kernels  45 us (96%)
  local copies, waits for them, and re-layouts  1.88 us (4%)
    pallas_call x1, Pallas kernels, fused(): pl.pallas_call(functools.partial(fused_kernel, ('row', 'col'), shape), ou...  45 us
    unnamed x1, local copies, waits for them, and re-layouts  1.88 us

profile of v5, /device:TPU:24, one launch (start us, length us, event | category | flops | bytes accessed | tf_op | source)
XLA Modules:
  0.0 46.9 jit_solution(13358063894455729861)
XLA Ops:
  0.0 45.0 %shard_map.37 = bf16[128,2048]{1,0:T(8,128)(2,1)} custom-call(bf16[128,2048]{1,0:T(8,128)(2,1)} %q_hbm.1, bf16[128,256]{1,0:T(8,128)(2,1)} %k_hbm.1, bf16[128,256]{1,0:T(8,128)(2,1)} %v_hbm.1), custom_call_target="tpu_custom_call" | custom-call | tf_op jit(solution)/shard_map/pallas_call | solution.py:357
  45.0 1.9 %copy.5 = bf16[128,2048]{1,0:T(8,128)(2,1)} copy(bf16[128,2048]{1,0:T(8,128)(2,1)} %shard_map.37) | data formatting | bytes 1048576
